TPU v7x, 128 devices: a whole 4x4x4 slice. The times are simulated.
128 devices in a mesh: blk: 32 (over y, z, x_lo), head: 4 (over x_hi, core).
Axes of the slice: x: 4 (x_hi: 2, x_lo: 2; x = x_hi * 2 + x_lo), y: 4, z: 4, core: 2. Of those that a mesh axis runs over, the one named last changes fastest.
Arguments:
- hidden_states: bfloat16 [16384, 4096], P('blk'), may hold values from -16 to 16
- w_query: bfloat16 [4096, 4096], P(None, 'head'), may hold values from -0.09375 to 0.09375
- key_matrix: bfloat16 [4096, 1024], P(None, 'head'), may hold values from -0.09375 to 0.09375
- value_matrix: bfloat16 [4096, 1024], P(None, 'head'), may hold values from -0.09375 to 0.09375
- w_out: bfloat16 [4096, 4096], P('head'), may hold values from -0.125 to 0.125
Outputs:
- attn_out: bfloat16 [16384, 4096], P('blk', 'head')
All inputs are finite; a program needn't handle non-finite values.
Results may differ from a plain program's by a relative error of at most 0.012.
Values may be sent and summed in bfloat16 or wider, within the bound.
A program may use at most 128 MiB of HBM per device.

v0:
```python
import jax
import jax.numpy as jnp
from jax import lax
from jax.sharding import PartitionSpec as P

HEAD_SIZE = 128


def broadcast(x, axis, root):
    mine = lax.axis_index(axis) == root
    return lax.psum(jnp.where(mine, x, jnp.zeros_like(x)), axis)


def apply_rotation(value_rows, token_positions, heads):
    token_rows = value_rows.shape[0]
    grid = value_rows.reshape(token_rows, heads, HEAD_SIZE)
    half = HEAD_SIZE // 2
    freqs = 500000.0 ** (-2.0 * jnp.arange(half, dtype=jnp.float32) / HEAD_SIZE)
    angle = token_positions[:, None] * freqs[None, :]
    cosine = jnp.cos(angle)[:, None, :]
    sine = jnp.sin(angle)[:, None, :]
    first = grid[:, :, :half]
    second = grid[:, :, half:]
    turned = jnp.concatenate(
        [first * cosine - second * sine, second * cosine + first * sine], axis=2
    )
    return turned.reshape(token_rows, heads * HEAD_SIZE).astype(jnp.bfloat16)


def project_pairs(tokens, key_matrix, value_matrix, token_positions):
    kv_heads = key_matrix.shape[1] // HEAD_SIZE
    key_rows = jnp.dot(tokens, key_matrix, preferred_element_type=jnp.float32)
    value_rows = jnp.dot(tokens, value_matrix, preferred_element_type=jnp.float32).astype(
        jnp.bfloat16
    )
    return (apply_rotation(key_rows, token_positions, kv_heads), value_rows)


def attend(
    query_rows, key_rows, value_rows, leading_block_keys, leading_block_values, anchor_on, kv_heads
):
    token_rows = query_rows.shape[0]
    repeat_heads = query_rows.shape[1] // (kv_heads * HEAD_SIZE)
    query_layout = query_rows.reshape(token_rows, kv_heads, repeat_heads, HEAD_SIZE)
    joined_keys = jnp.concatenate([leading_block_keys, key_rows], axis=0).reshape(
        2 * token_rows, kv_heads, HEAD_SIZE
    )
    joined_values = jnp.concatenate([leading_block_values, value_rows], axis=0).reshape(
        2 * token_rows, kv_heads, HEAD_SIZE
    )
    scores = jnp.einsum(
        "rgph,sgh->gprs", query_layout, joined_keys, preferred_element_type=jnp.float32
    )
    scores = scores / jnp.sqrt(jnp.float32(HEAD_SIZE))
    row_index = jnp.arange(token_rows)[:, None]
    col_index = jnp.arange(2 * token_rows)[None, :]
    visible = jnp.where(col_index < token_rows, anchor_on, col_index - token_rows <= row_index)
    scores = jnp.where(visible[None, None], scores, -jnp.inf)
    top = jnp.max(scores, axis=3, keepdims=True)
    expo = jnp.exp(scores - top)
    weights = (expo / jnp.sum(expo, axis=3, keepdims=True)).astype(jnp.bfloat16)
    context = jnp.einsum(
        "gprs,sgh->rgph", weights, joined_values, preferred_element_type=jnp.float32
    )
    return context.reshape(token_rows, query_rows.shape[1]).astype(jnp.bfloat16)


def local(hidden_states, w_query, key_matrix, value_matrix, w_out):
    token_rows = hidden_states.shape[0]
    block = lax.axis_index("blk")
    q_heads = w_query.shape[1] // HEAD_SIZE
    kv_heads = key_matrix.shape[1] // HEAD_SIZE
    token_positions = (block * token_rows + jnp.arange(token_rows, dtype=jnp.int32)).astype(
        jnp.float32
    )
    query_rows = apply_rotation(
        jnp.dot(hidden_states, w_query, preferred_element_type=jnp.float32),
        token_positions,
        q_heads,
    )
    key_rows, value_rows = project_pairs(hidden_states, key_matrix, value_matrix, token_positions)
    anchor_tokens = broadcast(hidden_states, "blk", 0)
    anchor_pos = jnp.arange(token_rows, dtype=jnp.float32)
    leading_block_keys, leading_block_values = project_pairs(
        anchor_tokens, key_matrix, value_matrix, anchor_pos
    )
    context = attend(
        query_rows,
        key_rows,
        value_rows,
        leading_block_keys,
        leading_block_values,
        block > 0,
        kv_heads,
    )
    partial_out = jnp.dot(context, w_out, preferred_element_type=jnp.float32)
    return lax.psum_scatter(partial_out, "head", scatter_dimension=1, tiled=True).astype(
        jnp.bfloat16
    )


def solution(mesh):
    in_specs = (P("blk", None), P(None, "head"), P(None, "head"), P(None, "head"), P("head", None))
    out_specs = P("blk", "head")
    return jax.shard_map(local, mesh=mesh, in_specs=in_specs, out_specs=out_specs, check_vma=False)
```

profile of v0, /device:TPU:18, one launch (start us, length us, event | category | flops | bytes accessed | tf_op | source)
XLA Modules:
  0.0 475.2 jit_solution(8182639195700875979)
XLA Ops:
  6.5 0.0 copy-start
  6.5 2.3 broadcast_select_fusion
  8.8 0.0 all-reduce.2.cloned.1.call-update
  8.8 0.0 reduce-scatter.2.cloned.1.call-start
  8.9 4.2 fusion.18
  13.1 0.2 copy.20
  13.3 1.0 copy.19
  14.3 8.1 %convolution_bitcast_fusion = f32[64,8,8,128]{3,1,2,0:T(8,128)S(1)} fusion(bf16[512,4096]{1,0:T(8,128)(2,1)} %param.5, bf16[4096,1024]{1,0:T(8,128)(2,1)} %param.6), kind=kOutput, calls=%fused_computation.15 | convolution fusion | flops 4294967296 | bytes 14680064 | tf_op jit(solution)/shard_map/dot_general | solution.py:77
  22.5 0.5 copy.21
  23.0 2.9 multiply_cosine_fusion
  25.9 0.9 subtract_convert_fusion
  26.7 0.0 copy-start.2
  26.8 0.6 pad_maximum_fusion
  27.3 1.1 copy.10
  28.5 1.5 fusion.6
  30.0 0.0 copy-done
  30.0 2.0 convolution_convert_fusion
  32.0 299.4 %all-reduce.2.cloned.1.call-done = bf16[512,4096]{1,0:T(8,128)(2,1)} async-done(((bf16[512,4096]{1,0:T(8,128)(2,1)}), bf16[512,4096]{1,0:T(8,128)(2,1)}) %all-reduce.2.cloned.1.call-update) | async-done | bytes 4194320 | tf_op jit(solution)/shard_map/psum | solution.py:11
  331.3 3.5 convolution_convert_fusion.1
  334.9 1.0 copy.16
  335.9 4.2 fusion.17
  340.2 0.2 copy.18
  340.4 0.2 copy.17
  340.6 0.0 copy-done.3
  340.6 0.0 copy-done.4
  340.6 1.1 subtract_convert_fusion.1
  341.7 10.9 %fusion.16 = (f32[2,4,512]{2,1,0:T(4,128)S(1)}, f32[2,4,512,1024]{2,3,1,0:T(8,128)}) fusion(pred[512,1024]{0,1:T(8,128)(4,1)} %fusion.6, bf16[512,2,4,128]{3,0,2,1:T(8,128)(2,1)} %bitcast.54, bf16[512,2,64]{2,0,1:T(8,128)(2,1)} %get-tuple-element.10, bf16[512,2,64]{2,0,1:T(8,128)(2,1)S(1)} %get-tuple-element.9, bf16[512,2,64]{2,0,1:T(8,128)(2,1)} %get-tuple-element.21, ...), kind=kOutput, calls=%fused_computation.39 | convolution fusion | flops 1092617216 | bytes 18890752 | tf_op jit(solution)/shard_map/sub | solution.py:60
  352.6 7.1 %fusion.9 = bf16[2,128,4,512]{3,1,2,0:T(8,128)(2,1)S(1)} fusion(bf16[1024,2,128,1]{0,2,3,1:T(8,128)(2,1)S(1)} %bitcast.55, f32[2,4,512,1024]{2,3,1,0:T(8,128)} %get-tuple-element.20, f32[2,4,512]{2,1,0:T(4,128)S(1)} %get-tuple-element.19), kind=kOutput, calls=%fused_computation.16 | convolution fusion | flops 1082654720 | bytes 18366464 | tf_op jit(solution)/shard_map/gprs,sgh->rgph/dot_general | solution.py:62
  359.7 10.2 %fusion.19 = f32[512,4096]{1,0:T(8,128)} fusion(bf16[512,1024]{0,1:T(8,128)(2,1)S(1)} %bitcast.53, bf16[1024,4096]{1,0:T(8,128)(2,1)} %param.9), kind=kOutput, calls=%fused_computation.42 | convolution fusion | flops 4294967296 | bytes 17825792 | tf_op jit(solution)/shard_map/dot_general | solution.py:96
  369.9 0.0 reduce-scatter.2.cloned.1.call-update
  369.9 95.8 %reduce-scatter.2.cloned.1.call-done = f32[512,1024]{1,0:T(8,128)} async-done(((f32[512,4096]{1,0:T(8,128)}), f32[512,1024]{1,0:T(8,128)}) %reduce-scatter.2.cloned.1.call-update) | async-done | bytes 2097168 | tf_op jit(solution)/shard_map/reduce_scatter | solution.py:97
  465.7 2.7 convert_element_type.45
  (17 shorter events, 0.2 us)
Async XLA Ops:
  6.5 23.5 %copy-start = (bf16[4096,256]{1,0:T(8,128)(2,1)S(1)}, bf16[4096,256]{1,0:T(8,128)(2,1)}, u32[]{:S(2)}) copy-start(bf16[4096,256]{1,0:T(8,128)(2,1)} %param.8) | copy-start | bytes 6291460
  6.5 324.8 %all-reduce.2.cloned.1.call-start = ((), (), s32[]{:S(2)}) async-start(), calls=%async_computation.1 | async-start | bytes 8388608 | tf_op jit(solution)/shard_map/psum | solution.py:11
  8.8 456.8 %reduce-scatter.2.cloned.1.call-start = ((), (), s32[]{:S(2)}) async-start(), calls=%async_computation.2 | async-start | bytes 10485760 | tf_op jit(solution)/shard_map/reduce_scatter | solution.py:97
  26.7 3.3 copy-start.2
  331.3 3.5 copy-start.6
  335.9 4.7 copy-start.3
  335.9 4.7 copy-start.4
  341.7 10.9 %copy-start.5 = (bf16[1024,256]{0,1:T(8,128)(2,1)S(1)}, bf16[1024,256]{0,1:T(8,128)(2,1)}, u32[]{:S(2)}) copy-start(bf16[1024,256]{0,1:T(8,128)(2,1)} %copy.16) | copy-start | bytes 1572868
  369.9 98.5 %copy-start.1 = (bf16[4096,256]{1,0:T(8,128)(2,1)S(1)}, bf16[4096,256]{1,0:T(8,128)(2,1)}, u32[]{:S(2)}) copy-start(bf16[4096,256]{1,0:T(8,128)(2,1)} %param.8) | copy-start | bytes 6291460
Sparse Core Ops, SparseCore 0:
  9.9 321.4 all-reduce.1
  370.0 95.5 reduce-scatter.1
where the time goes:
time: 477 us; the launch traced here: 475 us
  waiting for transfers between devices  395 us (83%)
  matrix products  50.2 us (11%)
  between operations  13.6 us (3%)
  other arithmetic  11.9 us (2%)
    psum x1, waiting for transfers between devices, broadcast(): return lax.psum(jnp.where(mine, x, jnp.zeros_like(x)), axis)  299 us
    reduce_scatter x1, waiting for transfers between devices, local(): lax.psum_scatter(partial_out, 'head', scatter_dimension=1, tiled=True)  95.8 us
    sub x1, matrix products, attend(): expo = jnp.exp(scores - top)  10.9 us
    dot_general x1, matrix products, local(): partial_out = jnp.dot(context, w_out, preferred_element_type=jnp.float32)  10.2 us
  transfers between devices with their start and end apart: 2, of which 2 were waited for; matrix products, arithmetic and copies ran while one was open for 5% of the time, Pallas kernels for 0%

commit v1 on v0

v1 whole, which is shorter than its diff:
```python
import jax
import jax.numpy as jnp
import numpy as np
from jax import lax
from jax.experimental import pallas as pl
from jax.experimental.pallas import tpu as pltpu
from jax.sharding import PartitionSpec as P

HEAD = 128
ROWS = 512
WIDTH = 4096
TILE = 128
TILES = ROWS // TILE
CHUNKS = 2
CROWS = ROWS // CHUNKS
PIECE = CROWS // 16
BODY = 256
MESH = pl.DeviceIdType.MESH
LOW = -1e30
F32 = jnp.float32
BF16 = jnp.bfloat16


def rotary_tables(blocks):
    half = HEAD // 2
    freqs = 500000.0 ** (-2.0 * np.arange(half) / HEAD)
    rows = np.arange(ROWS)[:, None] * freqs[None, :]
    starts = (np.arange(blocks) * ROWS)[:, None] * freqs[None, :]

    def both(x):
        return np.concatenate([x, x], axis=1).astype(np.float32)

    return (
        np.stack([both(np.cos(rows)), both(np.sin(rows))]),
        np.stack([both(np.cos(starts)), both(np.sin(starts))], axis=1),
    )


def dot(a, b):
    return jnp.dot(a, b, preferred_element_type=F32)


def dot_t(a, b):
    return lax.dot_general(a, b, (((1,), (1,)), ((), ())), preferred_element_type=F32)


def kernel(
    hid, wq, wk, wv, wo, row_tab, start_tab, out,
    hid_v, wq_v, wkv_v, wo_a, wo_b, rows_v, start_v, cos_v, sin_v,
    kvl, kva, q_v, vl_aug, va_aug, ol, ml, ctx, ctx_sib, acc_r, acc_l, sbuf, rbuf, obuf,
    hid_sem, wkv_sem, tab_sem, wq_sem, woa_sem, wob_send, wob_recv,
    sc_send, sc_recv, xl_send, xl_recv, ag_send, ag_recv,
    ctx_send, ctx_recv, x_send, x_recv, out_sem, own_sem,
):
    blk = lax.axis_index("blk")
    head = lax.axis_index("head")
    xl = lax.rem(blk, 2)
    pos = blk // 2
    y, z = pos // 4, lax.rem(pos, 4)
    xh, core = head // 2, lax.rem(head, 2)

    def plane(dy, dz):
        return ((lax.rem(y + dy, 4) * 4 + lax.rem(z + dz, 4)) * 2 + xl, head)

    peers = [plane(dy, dz) for dy in range(4) for dz in range(4) if (dy, dz) != (0, 0)]
    xl_peer = (pos * 2 + 1 - xl, head)
    sibling = (blk, xh * 2 + 1 - core)
    far_head = (1 - xh) * 2 + core
    far = (blk, far_head)

    barrier = pltpu.get_barrier_semaphore()
    friends = peers + [xl_peer, sibling, far]
    for friend in friends:
        pl.semaphore_signal(barrier, inc=1, device_id=friend, device_id_type=MESH)

    hid_cp = [
        pltpu.make_async_copy(
            hid.at[pl.ds(i * CROWS, CROWS)], hid_v.at[pl.ds(i * CROWS, CROWS)], hid_sem.at[i]
        )
        for i in range(CHUNKS)
    ]
    wk_cp = pltpu.make_async_copy(wk, wkv_v.at[:, pl.ds(0, 256)], wkv_sem.at[0])
    wv_cp = pltpu.make_async_copy(wv, wkv_v.at[:, pl.ds(256, 256)], wkv_sem.at[1])
    rows_cp = pltpu.make_async_copy(row_tab, rows_v, tab_sem.at[0])
    start_cp = pltpu.make_async_copy(start_tab, start_v, tab_sem.at[1])
    wq_cp = [
        pltpu.make_async_copy(wq.at[:, pl.ds(n * 256, 256)], wq_v.at[n], wq_sem.at[n])
        for n in range(4)
    ]
    woa_cp = [
        pltpu.make_async_copy(
            wo.at[:, pl.ds(pl.multiple_of(h * 1024, 1024), 1024)], wo_a.at[i], woa_sem.at[i]
        )
        for i, h in enumerate((far_head, head))
    ]
    hid_cp[0].start()
    wk_cp.start()
    wv_cp.start()
    start_cp.start()
    rows_cp.start()
    for cp in hid_cp[1:] + wq_cp:
        cp.start()

    start_cp.wait()
    rows_cp.wait()
    sign = jnp.where(lax.broadcasted_iota(jnp.int32, (TILE, HEAD), 1) < HEAD // 2, -1.0, 1.0)
    c0 = start_v[blk, 0:1, :]
    s0 = start_v[blk, 1:2, :]

    def make_tables(i, carry):
        rows = pl.ds(pl.multiple_of(i * TILE, TILE), TILE)
        cr, sr = rows_v[0, rows, :], rows_v[1, rows, :]
        cos_v[rows, :] = c0 * cr - s0 * sr
        sin_v[rows, :] = (s0 * cr + c0 * sr) * sign
        return carry

    lax.fori_loop(0, TILES, make_tables, 0)
    scale = float(np.log2(np.e) / np.sqrt(HEAD))

    def turn(x, c, s):
        return x * c + pltpu.roll(x, HEAD // 2, 1) * s

    def scatter(ch, i, target):
        rows = pl.ds(pl.multiple_of(ch * CROWS + i * PIECE, PIECE), PIECE)
        return pltpu.make_async_remote_copy(
            src_ref=kvl.at[rows], dst_ref=kva.at[rows], send_sem=sc_send.at[ch],
            recv_sem=sc_recv.at[ch], device_id=target, device_id_type=MESH,
        )

    def own_piece(ch):
        return pl.ds(pl.multiple_of(ch * CROWS + pos * PIECE, PIECE), PIECE)

    def forward(ch):
        rows = own_piece(ch)
        return pltpu.make_async_remote_copy(
            src_ref=kva.at[rows], dst_ref=kva.at[rows], send_sem=xl_send.at[ch],
            recv_sem=xl_recv.at[ch], device_id=xl_peer, device_id_type=MESH,
        )

    def gather(ch, target):
        rows = own_piece(ch)
        return pltpu.make_async_remote_copy(
            src_ref=kva.at[rows], dst_ref=kva.at[rows], send_sem=ag_send.at[ch],
            recv_sem=ag_recv.at[ch], device_id=target, device_id_type=MESH,
        )

    def own_copy(ch):
        rows = pl.ds(ch * CROWS, PIECE)
        return pltpu.make_async_copy(kvl.at[rows], kva.at[rows], own_sem.at[ch])

    def scatter_chunk(ch):
        @pl.when(blk == 0)
        def _():
            own_copy(ch).start()
            for dy in range(4):
                for dz in range(4):
                    if (dy, dz) != (0, 0):
                        scatter(ch, dy * 4 + dz, (jnp.int32((dy * 4 + dz) * 2), head)).start()

    def relay(ch, side):
        @pl.when(xl == side)
        def _():
            if side == 0:
                @pl.when(blk == 0)
                def _():
                    own_copy(ch).wait()

                @pl.when(blk != 0)
                def _():
                    scatter(ch, 0, sibling).wait_recv()

                forward(ch).start()
            else:
                forward(ch).wait_recv()
            for target in peers:
                gather(ch, target).start()

    wk_cp.wait()
    wv_cp.wait()
    for i in range(CHUNKS):
        hid_cp[i].wait()
        rows = pl.ds(i * CROWS, CROWS)
        kv = dot(hid_v[rows, :], wkv_v[...])
        c, s = cos_v[rows, :], sin_v[rows, :]
        for g in range(2):
            cols = slice(g * HEAD, (g + 1) * HEAD)
            kvl[rows, cols] = turn(kv[:, cols], c, s).astype(BF16)
        kvl[rows, 256:512] = kv[:, 256:512].astype(BF16)
        if i == 0:
            pl.semaphore_wait(barrier, len(friends))
        scatter_chunk(i)
    for g in range(2):
        vl_aug[g, :, 0:HEAD] = kvl[:, 256 + g * HEAD : 256 + (g + 1) * HEAD]
        vl_aug[g, :, HEAD:] = jnp.ones((ROWS, HEAD), BF16)
        va_aug[g, :, HEAD:] = jnp.ones((ROWS, HEAD), BF16)

    other = 1 - core
    wob_cp = [
        pltpu.make_async_remote_copy(
            src_ref=wo.at[:, pl.ds(pl.multiple_of(h * 1024, 1024), 1024)], dst_ref=wo_b.at[i],
            send_sem=wob_send.at[i], recv_sem=wob_recv.at[i],
            device_id=sibling, device_id_type=MESH,
        )
        for i, h in enumerate(((1 - xh) * 2 + other, xh * 2 + other))
    ]
    for cp in woa_cp + wob_cp:
        cp.start()

    for n in range(4):
        wq_cp[n].wait()
        g, j0 = n // 2, (n % 2) * 2

        def q_rows(m, carry, n=n, g=g, j0=j0):
            rows = pl.ds(pl.multiple_of(m * 256, 256), 256)
            x = dot(hid_v[rows, :], wq_v[n])
            c, s = cos_v[rows, :] * scale, sin_v[rows, :] * scale
            for j in range(2):
                turned = turn(x[:, j * HEAD : (j + 1) * HEAD], c, s).astype(BF16)
                for tt in range(2):
                    q_v[(2 * m + tt) * 2 + g, pl.ds((j0 + j) * TILE, TILE), :] = turned[
                        tt * TILE : (tt + 1) * TILE
                    ]
            return carry

        lax.fori_loop(0, 2, q_rows, 0)
        if n == 2:
            relay(0, 0)
    relay(1, 0)

    def local_tile(t):
        keys = (t + 1) * TILE
        diag = (
            lax.broadcasted_iota(jnp.int32, (BODY, keys), 1) - t * TILE
            <= lax.rem(lax.broadcasted_iota(jnp.int32, (BODY, keys), 0), TILE)
        )
        for g in range(2):
            def body(b, carry, g=g):
                rows = pl.ds(pl.multiple_of(b * BODY, BODY), BODY)
                s = dot_t(q_v[t * 2 + g, rows, :], kvl[0:keys, g * HEAD : (g + 1) * HEAD])
                s = jnp.where(diag, s, LOW)
                top = jnp.max(s, axis=1, keepdims=True)
                p = jnp.exp2(s - top).astype(BF16)
                ol[t * 2 + g, rows, :] = dot(p, vl_aug[g, 0:keys, :])
                ml[t * 2 + g, rows, :] = jnp.broadcast_to(top, (BODY, HEAD))
                return carry

            lax.fori_loop(0, ROWS // BODY, body, 0)

    local_tile(0)
    local_tile(1)
    relay(0, 1)
    local_tile(2)
    relay(1, 1)
    local_tile(3)

    got = pl.ds(0, 15 * PIECE)
    for ch in range(CHUNKS):
        pltpu.make_async_copy(kva.at[got], kva.at[got], ag_recv.at[ch]).wait()
    for g in range(2):
        va_aug[g, :, 0:HEAD] = kva[:, 256 + g * HEAD : 256 + (g + 1) * HEAD]

    def ctx_copy(t, g):
        cols = pl.ds(g * 512, 512)
        return pltpu.make_async_remote_copy(
            src_ref=ctx.at[t, :, cols], dst_ref=ctx_sib.at[t, :, cols],
            send_sem=ctx_send.at[t, g], recv_sem=ctx_recv.at[t, g],
            device_id=sibling, device_id_type=MESH,
        )

    def x_copy(t):
        return pltpu.make_async_remote_copy(
            src_ref=sbuf.at[t], dst_ref=rbuf.at[t], send_sem=x_send.at[t],
            recv_sem=x_recv.at[t], device_id=far, device_id_type=MESH,
        )

    has_anchor = blk > 0
    for t in range(TILES):
        for g in range(2):
            for b in range(ROWS // BODY):
                rows = slice(b * BODY, (b + 1) * BODY)
                s = dot_t(q_v[t * 2 + g, rows, :], kva[:, g * HEAD : (g + 1) * HEAD])
                before = ml[t * 2 + g, rows, :][:, 0:1]
                both = jnp.maximum(jnp.max(s, axis=1, keepdims=True), before)
                top = jnp.where(has_anchor, both, before)
                p = jnp.exp2(s - jnp.where(has_anchor, both, -LOW)).astype(BF16)
                o = dot(p, va_aug[g]) + ol[t * 2 + g, rows, :] * jnp.exp2(before - top)
                res = (o[:, 0:HEAD] / o[:, HEAD:]).astype(BF16)
                for j in range(BODY // TILE):
                    col = (g * 4 + b * (BODY // TILE) + j) * HEAD
                    ctx[t, :, col : col + HEAD] = res[j * TILE : (j + 1) * TILE]
            ctx_copy(t, g).start()
        if t == 0:
            for cp in woa_cp:
                cp.wait()

        def own_part(n, carry, t=t):
            cols = pl.ds(pl.multiple_of(n * 256, 256), 256)
            acc_r[:, cols] = dot(ctx[t], wo_a[0, :, cols])
            acc_l[t, :, cols] = dot(ctx[t], wo_a[1, :, cols])
            return carry

        lax.fori_loop(0, 4, own_part, 0)
        if t == 0:
            for cp in wob_cp:
                cp.wait_recv()
        for g in range(2):
            ctx_copy(t, g).wait_recv()

        def far_part(n, carry, t=t):
            cols = pl.ds(pl.multiple_of(n * 256, 256), 256)
            sbuf[t, :, cols] = (acc_r[:, cols] + dot(ctx_sib[t], wo_b[0, :, cols])).astype(BF16)
            return carry

        lax.fori_loop(0, 4, far_part, 0)
        x_copy(t).start()

        def near_part(n, carry, t=t):
            cols = pl.ds(pl.multiple_of(n * 256, 256), 256)
            acc_l[t, :, cols] += dot(ctx_sib[t], wo_b[1, :, cols])
            return carry

        lax.fori_loop(0, 4, near_part, 0)

    out_cp = [
        pltpu.make_async_copy(obuf.at[t], out.at[pl.ds(t * TILE, TILE)], out_sem.at[t])
        for t in range(TILES)
    ]
    for t in range(TILES):
        x_copy(t).wait_recv()
        obuf[t] = (acc_l[t] + rbuf[t].astype(F32)).astype(BF16)
        out_cp[t].start()

    for cp in wob_cp:
        cp.wait_send()
    for ch in range(CHUNKS):
        @pl.when(blk == 0)
        def _(ch=ch):
            pltpu.make_async_copy(kvl.at[got], kvl.at[got], sc_send.at[ch]).wait()

        @pl.when(xl == 0)
        def _(ch=ch):
            forward(ch).wait_send()

        pltpu.make_async_copy(kva.at[got], kva.at[got], ag_send.at[ch]).wait()
    for t in range(TILES):
        for g in range(2):
            ctx_copy(t, g).wait_send()
        x_copy(t).wait_send()
        out_cp[t].wait()


def local(hidden_states, w_query, key_matrix, value_matrix, w_out):
    row_tab, start_tab = rotary_tables(32)
    any_spec = pl.BlockSpec(memory_space=pl.ANY)
    dma = pltpu.SemaphoreType.DMA
    return pl.pallas_call(
        kernel,
        out_shape=jax.ShapeDtypeStruct((ROWS, 1024), BF16),
        in_specs=[any_spec] * 7,
        out_specs=any_spec,
        scratch_shapes=[
            pltpu.VMEM((ROWS, WIDTH), BF16),
            pltpu.VMEM((4, WIDTH, 256), BF16),
            pltpu.VMEM((WIDTH, 512), BF16),
            pltpu.VMEM((2, 1024, 1024), BF16),
            pltpu.VMEM((2, 1024, 1024), BF16),
            pltpu.VMEM((2, ROWS, HEAD), F32),
            pltpu.VMEM((32, 2, HEAD), F32),
            pltpu.VMEM((ROWS, HEAD), F32),
            pltpu.VMEM((ROWS, HEAD), F32),
            pltpu.VMEM((ROWS, 512), BF16),
            pltpu.VMEM((ROWS, 512), BF16),
            pltpu.VMEM((TILES * 2, 4 * TILE, HEAD), BF16),
            pltpu.VMEM((2, ROWS, 2 * HEAD), BF16),
            pltpu.VMEM((2, ROWS, 2 * HEAD), BF16),
            pltpu.VMEM((TILES * 2, 4 * TILE, 2 * HEAD), F32),
            pltpu.VMEM((TILES * 2, 4 * TILE, HEAD), F32),
            pltpu.VMEM((TILES, TILE, 1024), BF16),
            pltpu.VMEM((TILES, TILE, 1024), BF16),
            pltpu.VMEM((TILE, 1024), F32),
            pltpu.VMEM((TILES, TILE, 1024), F32),
            pltpu.VMEM((TILES, TILE, 1024), BF16),
            pltpu.VMEM((TILES, TILE, 1024), BF16),
            pltpu.VMEM((TILES, TILE, 1024), BF16),
            dma((CHUNKS,)), dma((2,)), dma((2,)), dma((4,)), dma((2,)), dma((2,)), dma((2,)),
            dma((CHUNKS,)), dma((CHUNKS,)), dma((CHUNKS,)), dma((CHUNKS,)),
            dma((CHUNKS,)), dma((CHUNKS,)),
            dma((TILES, 2)), dma((TILES, 2)), dma((TILES,)), dma((TILES,)), dma((TILES,)),
            dma((CHUNKS,)),
        ],
        compiler_params=pltpu.CompilerParams(
            collective_id=0, has_side_effects=True, vmem_limit_bytes=60 * 2**20
        ),
        name="layer",
    )(
        hidden_states, w_query, key_matrix, value_matrix, w_out,
        jnp.asarray(row_tab), jnp.asarray(start_tab),
    )


def solution(mesh):
    in_specs = (P("blk", None), P(None, "head"), P(None, "head"), P(None, "head"), P("head", None))
    out_specs = P("blk", "head")
    return jax.shard_map(local, mesh=mesh, in_specs=in_specs, out_specs=out_specs, check_vma=False)
```

time: 477 us -> 63.5 us (0.13)
  the two profiles are of different devices: /device:TPU:18 before, /device:TPU:2 now
where the time goes in v1:
time: 63.5 us; the launch traced here: 63.4 us
  Pallas kernels  61.1 us (96%)
  local copies, waits for them, and re-layouts  2.26 us (4%)
    pallas_call x1, Pallas kernels, local(): pl.pallas_call(kernel, out_shape=jax.ShapeDtypeStruct((ROWS, 1024), BF16)...  61.1 us
    unnamed x1, local copies, waits for them, and re-layouts  2.26 us

profile of v1, /device:TPU:2, one launch (start us, length us, event | category | flops | bytes accessed | tf_op | source)
XLA Modules:
  0.0 63.4 jit_solution(7333388318749179055)
XLA Ops:
  0.0 61.1 %layer.1 = bf16[512,1024]{1,0:T(8,128)(2,1)} custom-call(bf16[512,4096]{1,0:T(8,128)(2,1)} %hid.1, bf16[4096,1024]{1,0:T(8,128)(2,1)} %wq.1, bf16[4096,256]{1,0:T(8,128)(2,1)} %wk.1, bf16[4096,256]{1,0:T(8,128)(2,1)} %wv.1, bf16[1024,4096]{1,0:T(8,128)(2,1)} %wo.1, f32[2,512,128]{2,1,0:T(8,128)} %constant.4.clone.row_tab, f32[32,2,128]{2,1,0:T(2,128)} %constant.5.clone.start_tab), custom_call_target="tpu_custom_call" | custom-call | tf_op jit(solution)/shard_map/layer/pallas_call | solution.py:356
  61.1 2.3 %copy.9 = bf16[512,1024]{1,0:T(8,128)(2,1)} copy(bf16[512,1024]{1,0:T(8,128)(2,1)} %layer.1) | data formatting | bytes 2097152

commit v2 on v1

v2 whole, which is shorter than its diff:
```python
import jax
import jax.numpy as jnp
import numpy as np
from jax import lax
from jax.experimental import pallas as pl
from jax.experimental.pallas import tpu as pltpu
from jax.sharding import PartitionSpec as P

HEAD = 128
ROWS = 512
WIDTH = 4096
TILE = 128
TILES = ROWS // TILE
CHUNKS = 2
CROWS = ROWS // CHUNKS
PIECE = CROWS // 8
BODY = 256
MESH = pl.DeviceIdType.MESH
LOW = -1e30
F32 = jnp.float32
BF16 = jnp.bfloat16


def rotary_tables(blocks):
    freqs = 500000.0 ** (-2.0 * np.arange(HEAD // 2) / HEAD)

    def table(tokens):
        angle = tokens[..., None] * freqs
        both = [np.concatenate([f(angle)] * 2, axis=-1) for f in (np.cos, np.sin)]
        return np.stack(both, axis=-3).astype(np.float32)

    return table(np.arange(blocks * ROWS // 16).reshape(blocks, -1) * 16.0), table(np.arange(16.0))


def dot(a, b):
    return jnp.dot(a, b, preferred_element_type=F32)


def dot_t(a, b):
    return lax.dot_general(a, b, (((1,), (1,)), ((), ())), preferred_element_type=F32)


def kernel(
    hid, wq, wk, wv, wo, coarse_tab, fine_tab, out,
    hid_v, wq_v, wkv_v, wo_a, wo_b, coarse, fine, cos_v, sin_v,
    kv_acc, kvl, kva, stage, q_v, vl_aug, va_aug, ol, ml, ctx, ctx_sib, acc_r, acc_l, sbuf, rbuf,
    hid_sem, wkv_sem, tab_sem, wq_sem, woa_sem, wob_send, wob_recv,
    first_send, aside_send, mine_recv, ring_send, fwd_send, rest_send, home_send, rest_recv,
    ctx_send, ctx_recv, x_send, x_recv, own_sem,
):
    blk = lax.axis_index("blk")
    head = lax.axis_index("head")
    xl = lax.rem(blk, 2)
    pos = blk // 2
    y, z = pos // 4, lax.rem(pos, 4)
    xh, core = head // 2, lax.rem(head, 2)

    def along(part, d):
        if part == 0:
            return (lax.rem(y + d, 4) * 4 + z) * 2 + xl
        return (y * 4 + lax.rem(z + d, 4)) * 2 + xl

    rings = [[along(part, d) for d in (1, 2, 3)] for part in range(2)]
    xl_peer = pos * 2 + 1 - xl
    zero, one = xh * 2, xh * 2 + 1
    sibling = (blk, xh * 2 + 1 - core)
    far_head = (1 - xh) * 2 + core
    far = (blk, far_head)

    barrier = pltpu.get_barrier_semaphore()
    friends = [(b, h) for b in rings[0] + rings[1] for h in (zero, one)]
    friends += [(xl_peer, head), sibling, far]
    for friend in friends:
        pl.semaphore_signal(barrier, inc=1, device_id=friend, device_id_type=MESH)

    hid_cp = [
        pltpu.make_async_copy(
            hid.at[pl.ds(0, CROWS), pl.ds(d * 2048, 2048)],
            hid_v.at[pl.ds(0, CROWS), pl.ds(d * 2048, 2048)],
            hid_sem.at[d],
        )
        for d in range(2)
    ]
    later_cp = pltpu.make_async_copy(
        hid.at[pl.ds(CROWS, CROWS)], hid_v.at[pl.ds(CROWS, CROWS)], hid_sem.at[2]
    )
    half = WIDTH // 2
    wkv_cp = [
        pltpu.make_async_copy(
            w.at[pl.ds(d * half, half)],
            wkv_v.at[pl.ds(d * half, half), pl.ds(i * 256, 256)],
            wkv_sem.at[d, i],
        )
        for d in range(2)
        for i, w in enumerate((wk, wv))
    ]
    tab_cp = [
        pltpu.make_async_copy(coarse_tab.at[blk], coarse, tab_sem.at[0]),
        pltpu.make_async_copy(fine_tab, fine, tab_sem.at[1]),
    ]
    wq_cp = [
        pltpu.make_async_copy(wq.at[:, pl.ds(n * 512, 512)], wq_v.at[n], wq_sem.at[n])
        for n in range(2)
    ]
    woa_cp = [
        pltpu.make_async_copy(
            wo.at[:, pl.ds(pl.multiple_of(h * 1024, 1024), 1024)], wo_a.at[i], woa_sem.at[i]
        )
        for i, h in enumerate((far_head, head))
    ]
    first_half = [hid_cp[0], wkv_cp[0], wkv_cp[1]]
    second_half = [hid_cp[1], wkv_cp[2], wkv_cp[3]]
    for cp in tab_cp + first_half + second_half + [later_cp]:
        cp.start()
    def make_tables():
        lane = lax.broadcasted_iota(jnp.int32, (16, HEAD), 1)
        sign = jnp.where(lane < HEAD // 2, -1.0, 1.0)
        cf, sf = fine[0], fine[1]

        def step(i, carry):
            ca, sa = coarse[0, pl.ds(i, 1), :], coarse[1, pl.ds(i, 1), :]
            rows = pl.ds(pl.multiple_of(i * 16, 16), 16)
            cos_v[rows, :] = ca * cf - sa * sf
            sin_v[rows, :] = (sa * cf + ca * sf) * sign
            return carry

        lax.fori_loop(0, ROWS // 16, step, 0, unroll=4)

    scale = float(np.log2(np.e) / np.sqrt(HEAD))

    def turn(x, c, s):
        return x * c + pltpu.roll(x, HEAD // 2, 1) * s

    lines = (y, z)
    held = (stage, kva)

    def piece(ch, part, j):
        return pl.ds(pl.multiple_of(ch * CROWS + (part * 4 + j) * PIECE, PIECE), PIECE)

    def push(src, dst, ch, part, j, send_sem, recv_sem, target):
        rows = piece(ch, part, j)
        return pltpu.make_async_remote_copy(
            src_ref=src.at[rows], dst_ref=dst.at[rows], send_sem=send_sem, recv_sem=recv_sem,
            device_id=target, device_id_type=MESH,
        )

    def own_copy(ch, part):
        rows = piece(ch, part, 0)
        return pltpu.make_async_copy(kvl.at[rows], kva.at[rows], own_sem.at[ch, part])

    def aside(ch, part):
        return push(
            kvl, stage, ch, part, 0, aside_send.at[ch, part], mine_recv.at[ch, part, 0], sibling
        )

    def first(ch, part, d, grp):
        return push(
            kvl, held[grp], ch, part, d, first_send.at[ch], mine_recv.at[ch, part, grp],
            (rings[part][d - 1], one),
        )

    def forward(ch, part, grp):
        return push(
            held[grp], held[grp], ch, part, lines[part], fwd_send.at[ch, part, grp],
            mine_recv.at[ch, part, grp], (xl_peer, one),
        )

    def across(ch, part, d, grp):
        return push(
            held[grp], held[grp], ch, part, lines[part], ring_send.at[ch, part, grp],
            mine_recv.at[ch, part, grp], (rings[1 - part][d - 1], one),
        )

    def rest(ch, part, d, grp):
        return push(
            held[grp], kva, ch, part, lines[part], rest_send.at[ch, grp], rest_recv.at[ch],
            (rings[part][d - 1], (zero, one)[grp]),
        )

    def home(ch, part):
        return push(
            stage, kva, ch, part, lines[part], home_send.at[ch, part], rest_recv.at[ch], sibling
        )

    def scatter_chunk(ch):
        for grp in range(2):
            @pl.when(jnp.logical_and(blk == 0, core == grp))
            def _(grp=grp):
                for part in range(2):
                    for d in (1, 2, 3):
                        first(ch, part, d, grp).start()
                for part in range(2):
                    if grp == 0:
                        aside(ch, part).start()
                    else:
                        own_copy(ch, part).start()

    def relay_part(ch, part, early):
        at_root = lines[1 - part] == 0

        @pl.when(at_root if early else jnp.logical_not(at_root))
        def _():
            forward(ch, part, 0).wait_recv()
            if early:
                @pl.when(blk == 0)
                def _():
                    own_copy(ch, part).wait()

                @pl.when(blk != 0)
                def _():
                    forward(ch, part, 1).wait_recv()
            else:
                forward(ch, part, 1).wait_recv()
            if early:
                for grp in range(2):
                    @pl.when(xl == 0)
                    def _(grp=grp):
                        forward(ch, part, grp).start()

                    for d in (1, 2, 3):
                        across(ch, part, d, grp).start()
            else:
                send_rest(ch, part)

    def send_rest(ch, part):
        for grp in range(2):
            for d in (1, 2, 3):
                rest(ch, part, d, grp).start()
        home(ch, part).start()

    def root_rest(side):
        for part in range(2):
            mine = jnp.logical_and(lines[1 - part] == 0, xl == side)

            @pl.when(jnp.logical_and(mine, core == 1))
            def _(part=part):
                for ch in range(CHUNKS):
                    send_rest(ch, part)

    def relay(ch, side, early):
        @pl.when(jnp.logical_and(xl == side, core == 1))
        def _():
            for part in range(2):
                relay_part(ch, part, early)

    for cp in first_half:
        cp.wait()
    for i in range(CHUNKS):
        rows = pl.ds(i * CROWS, CROWS)
        if i == 0:
            kv_acc[...] = dot(hid_v[rows, 0:half], wkv_v[0:half, :])
            for cp in second_half:
                cp.wait()
            for cp in wq_cp:
                cp.start()
            kv_acc[...] += dot(hid_v[rows, half:], wkv_v[half:, :])
            for cp in tab_cp:
                cp.wait()
            make_tables()
            kv = kv_acc[...]
        else:
            later_cp.wait()
            kv = dot(hid_v[rows, :], wkv_v[...])
        c, s = cos_v[rows, :], sin_v[rows, :]
        for g in range(2):
            cols = slice(g * HEAD, (g + 1) * HEAD)
            kvl[rows, cols] = turn(kv[:, cols], c, s).astype(BF16)
        kvl[rows, 256:512] = kv[:, 256:512].astype(BF16)
    pl.semaphore_wait(barrier, len(friends))
    for ch in range(CHUNKS):
        scatter_chunk(ch)
    for g in range(2):
        vl_aug[g, :, 0:HEAD] = kvl[:, 256 + g * HEAD : 256 + (g + 1) * HEAD]
        vl_aug[g, :, HEAD:] = jnp.ones((ROWS, HEAD), BF16)
        va_aug[g, :, HEAD:] = jnp.ones((ROWS, HEAD), BF16)

    other = 1 - core
    wob_cp = [
        pltpu.make_async_remote_copy(
            src_ref=wo.at[:, pl.ds(pl.multiple_of(h * 1024, 1024), 1024)], dst_ref=wo_b.at[i],
            send_sem=wob_send.at[i], recv_sem=wob_recv.at[i],
            device_id=sibling, device_id_type=MESH,
        )
        for i, h in enumerate(((1 - xh) * 2 + other, xh * 2 + other))
    ]
    for cp in woa_cp + wob_cp:
        cp.start()

    relay(0, 0, True)
    relay(1, 0, True)
    for n in range(4):
        g, m = n // 2, n % 2
        if m == 0:
            wq_cp[g].wait()
        x = dot(hid_v[m * 256 : (m + 1) * 256, :], wq_v[g])
        rows = slice(m * 256, (m + 1) * 256)
        c, s = cos_v[rows, :] * scale, sin_v[rows, :] * scale
        for j in range(4):
            turned = turn(x[:, j * HEAD : (j + 1) * HEAD], c, s).astype(BF16)
            for tt in range(2):
                q_v[(2 * m + tt) * 2 + g, j * TILE : (j + 1) * TILE, :] = turned[
                    tt * TILE : (tt + 1) * TILE
                ]
        if n == 1:
            root_rest(0)
        if n == 2:
            relay(0, 1, True)
            relay(1, 1, True)
            relay(0, 0, False)
            relay(1, 0, False)
        if n == 3:
            root_rest(1)

    diag = lax.broadcasted_iota(jnp.int32, (BODY, TILE), 1) <= lax.rem(
        lax.broadcasted_iota(jnp.int32, (BODY, TILE), 0), TILE
    )
    bodies = [(g, b) for g in range(2) for b in range(ROWS // BODY)]

    def local_scores(t, g, b):
        q = q_v[t * 2 + g, b * BODY : (b + 1) * BODY, :]
        return dot_t(q, kvl[0 : (t + 1) * TILE, g * HEAD : (g + 1) * HEAD])

    def local_finish(t, g, b, s):
        rows = slice(b * BODY, (b + 1) * BODY)
        last = jnp.where(diag, s[:, t * TILE :], LOW)
        s = last if t == 0 else jnp.concatenate([s[:, : t * TILE], last], axis=1)
        top = jnp.max(s, axis=1, keepdims=True)
        p = jnp.exp2(s - top).astype(BF16)
        ol[t * 2 + g, rows, :] = dot(p, vl_aug[g, 0 : (t + 1) * TILE, :])
        ml[t * 2 + g, rows, :] = jnp.broadcast_to(top, (BODY, HEAD))

    def local_tile(t):
        s = local_scores(t, *bodies[0])
        for k, (g, b) in enumerate(bodies):
            ahead = local_scores(t, *bodies[k + 1]) if k + 1 < len(bodies) else None
            local_finish(t, g, b, s)
            s = ahead

    local_tile(1)
    local_tile(2)
    relay(0, 1, False)
    relay(1, 1, False)
    local_tile(3)

    got, eight = pl.ds(0, 6 * PIECE), pl.ds(0, 8 * PIECE)

    def anchor_here(ch):
        @pl.when(core == 1)
        def _():
            pltpu.make_async_copy(kva.at[got], kva.at[got], rest_recv.at[ch]).wait()

        @pl.when(core == 0)
        def _():
            pltpu.make_async_copy(kva.at[eight], kva.at[eight], rest_recv.at[ch]).wait()

        rows = pl.ds(ch * CROWS, CROWS)
        for g in range(2):
            va_aug[g, rows, 0:HEAD] = kva[rows, 256 + g * HEAD : 256 + (g + 1) * HEAD]

    def ctx_copy(t, g):
        cols = pl.ds(g * 512, 512)
        return pltpu.make_async_remote_copy(
            src_ref=ctx.at[t, :, cols], dst_ref=ctx_sib.at[t, :, cols],
            send_sem=ctx_send.at[t, g], recv_sem=ctx_recv.at[t, g],
            device_id=sibling, device_id_type=MESH,
        )

    def x_copy(t, c):
        cols = pl.ds(c * 512, 512)
        return pltpu.make_async_remote_copy(
            src_ref=sbuf.at[t, :, cols], dst_ref=rbuf.at[t, :, cols],
            send_sem=x_send.at[t, c], recv_sem=x_recv.at[t, c],
            device_id=far, device_id_type=MESH,
        )

    has_anchor = blk > 0

    def early_scores(g, b):
        q = q_v[g, b * BODY : (b + 1) * BODY, :]
        cols = slice(g * HEAD, (g + 1) * HEAD)
        return dot_t(q, kva[0:CROWS, cols]), dot_t(q, kvl[0:TILE, cols])

    def early_finish(g, b, s):
        rows = slice(b * BODY, (b + 1) * BODY)
        s = jnp.concatenate(
            [jnp.where(has_anchor, s[0], LOW), jnp.where(diag, s[1], LOW)], axis=1
        )
        top = jnp.max(s, axis=1, keepdims=True)
        p = jnp.exp2(s - top).astype(BF16)
        ol[g, rows, :] = dot(p[:, 0:CROWS], va_aug[g, 0:CROWS, :]) + dot(
            p[:, CROWS:], vl_aug[g, 0:TILE, :]
        )
        ml[g, rows, :] = jnp.broadcast_to(top, (BODY, HEAD))

    anchor_here(0)
    s = early_scores(*bodies[0])
    for k, (g, b) in enumerate(bodies):
        ahead = early_scores(*bodies[k + 1]) if k + 1 < len(bodies) else None
        early_finish(g, b, s)
        s = ahead
    anchor_here(1)

    def anchor_scores(t, g, b):
        q = q_v[t * 2 + g, b * BODY : (b + 1) * BODY, :]
        return dot_t(q, kva[0 if t else CROWS : ROWS, g * HEAD : (g + 1) * HEAD])

    def anchor_finish(t, g, b, s):
        rows = slice(b * BODY, (b + 1) * BODY)
        before = ml[t * 2 + g, rows, :][:, 0:1]
        both = jnp.maximum(jnp.max(s, axis=1, keepdims=True), before)
        top = jnp.where(has_anchor, both, before)
        p = jnp.exp2(s - jnp.where(has_anchor, both, -LOW)).astype(BF16)
        o = dot(p, va_aug[g, 0 if t else CROWS : ROWS, :]) + ol[t * 2 + g, rows, :] * jnp.exp2(before - top)
        res = (o[:, 0:HEAD] / o[:, HEAD:]).astype(BF16)
        for j in range(BODY // TILE):
            col = (g * 4 + b * (BODY // TILE) + j) * HEAD
            ctx[t, :, col : col + HEAD] = res[j * TILE : (j + 1) * TILE]

    def anchor_tile(t):
        s = anchor_scores(t, *bodies[0])
        for k, (g, b) in enumerate(bodies):
            ahead = anchor_scores(t, *bodies[k + 1]) if k + 1 < len(bodies) else None
            anchor_finish(t, g, b, s)
            s = ahead
            if b == ROWS // BODY - 1:
                ctx_copy(t, g).start()

    def near_part(t):
        acc_l[t] = dot(ctx[t], wo_a[1]) + dot(ctx_sib[t], wo_b[1])

    def sibling_here(t):
        for g in range(2):
            ctx_copy(t, g).wait_recv()

    anchor_tile(0)
    for cp in woa_cp:
        cp.wait()
    acc_r[...] = dot(ctx[0], wo_a[0])
    for cp in wob_cp:
        cp.wait_recv()
    sibling_here(0)
    for c in range(2):
        cols = slice(c * 512, (c + 1) * 512)
        sbuf[0, :, cols] = (acc_r[:, cols] + dot(ctx_sib[0], wo_b[0, :, cols])).astype(BF16)
        x_copy(0, c).start()
    for t in range(1, TILES):
        anchor_tile(t)
        near_part(t - 1)
        sibling_here(t)
        for c in range(2):
            cols = slice(c * 512, (c + 1) * 512)
            sbuf[t, :, cols] = (
                dot(ctx[t], wo_a[0, :, cols]) + dot(ctx_sib[t], wo_b[0, :, cols])
            ).astype(BF16)
            x_copy(t, c).start()
    near_part(TILES - 1)

    for t in range(TILES):
        for c in range(2):
            cols = slice(c * 512, (c + 1) * 512)
            x_copy(t, c).wait_recv()
            out[pl.ds(t * TILE, TILE), cols] = (
                acc_l[t, :, cols] + rbuf[t, :, cols].astype(F32)
            ).astype(BF16)

    for cp in wob_cp:
        cp.wait_send()
    for ch in range(CHUNKS):
        @pl.when(blk == 0)
        def _(ch=ch):
            pltpu.make_async_copy(kvl.at[got], kvl.at[got], first_send.at[ch]).wait()

            @pl.when(core == 0)
            def _():
                for part in range(2):
                    aside(ch, part).wait_send()

        @pl.when(core == 1)
        def _(ch=ch):
            for part in range(2):
                @pl.when(lines[1 - part] == 0)
                def _(part=part):
                    three = pl.ds(0, 3 * PIECE)
                    for grp in range(2):
                        pltpu.make_async_copy(
                            kva.at[three], kva.at[three], ring_send.at[ch, part, grp]
                        ).wait()

                        @pl.when(xl == 0)
                        def _(grp=grp):
                            forward(ch, part, grp).wait_send()

                home(ch, part).wait_send()
            for grp in range(2):
                pltpu.make_async_copy(kva.at[got], kva.at[got], rest_send.at[ch, grp]).wait()

    for t in range(TILES):
        for g in range(2):
            ctx_copy(t, g).wait_send()
            x_copy(t, g).wait_send()


def local(hidden_states, w_query, key_matrix, value_matrix, w_out):
    coarse_tab, fine_tab = rotary_tables(32)
    any_spec = pl.BlockSpec(memory_space=pl.ANY)
    dma = pltpu.SemaphoreType.DMA
    return pl.pallas_call(
        kernel,
        out_shape=pltpu.VMEM((ROWS, 1024), BF16),
        in_specs=[any_spec] * 7,
        out_specs=pl.BlockSpec(memory_space=pltpu.VMEM),
        scratch_shapes=[
            pltpu.VMEM((ROWS, WIDTH), BF16),
            pltpu.VMEM((2, WIDTH, 512), BF16),
            pltpu.VMEM((WIDTH, 512), BF16),
            pltpu.VMEM((2, 1024, 1024), BF16),
            pltpu.VMEM((2, 1024, 1024), BF16),
            pltpu.VMEM((2, ROWS // 16, HEAD), F32),
            pltpu.VMEM((2, 16, HEAD), F32),
            pltpu.VMEM((ROWS, HEAD), F32),
            pltpu.VMEM((ROWS, HEAD), F32),
            pltpu.VMEM((CROWS, 512), F32),
            pltpu.VMEM((ROWS, 512), BF16),
            pltpu.VMEM((ROWS, 512), BF16),
            pltpu.VMEM((ROWS, 512), BF16),
            pltpu.VMEM((TILES * 2, 4 * TILE, HEAD), BF16),
            pltpu.VMEM((2, ROWS, 2 * HEAD), BF16),
            pltpu.VMEM((2, ROWS, 2 * HEAD), BF16),
            pltpu.VMEM((TILES * 2, 4 * TILE, 2 * HEAD), F32),
            pltpu.VMEM((TILES * 2, 4 * TILE, HEAD), F32),
            pltpu.VMEM((TILES, TILE, 1024), BF16),
            pltpu.VMEM((TILES, TILE, 1024), BF16),
            pltpu.VMEM((TILE, 1024), F32),
            pltpu.VMEM((TILES, TILE, 1024), F32),
            pltpu.VMEM((TILES, TILE, 1024), BF16),
            pltpu.VMEM((TILES, TILE, 1024), BF16),
            dma((3,)), dma((2, 2)), dma((2,)), dma((2,)), dma((2,)), dma((2,)), dma((2,)),
            dma((CHUNKS,)), dma((CHUNKS, 2)), dma((CHUNKS, 2, 2)), dma((CHUNKS, 2, 2)),
            dma((CHUNKS, 2, 2)), dma((CHUNKS, 2)), dma((CHUNKS, 2)), dma((CHUNKS,)),
            dma((TILES, 2)), dma((TILES, 2)), dma((TILES, 2)), dma((TILES, 2)),
            dma((CHUNKS, 2)),
        ],
        compiler_params=pltpu.CompilerParams(
            collective_id=0, has_side_effects=True, vmem_limit_bytes=60 * 2**20
        ),
        name="layer",
    )(
        hidden_states, w_query, key_matrix, value_matrix, w_out,
        jnp.asarray(coarse_tab), jnp.asarray(fine_tab),
    )


def solution(mesh):
    in_specs = (P("blk", None), P(None, "head"), P(None, "head"), P(None, "head"), P("head", None))
    out_specs = P("blk", "head")
    return jax.shard_map(local, mesh=mesh, in_specs=in_specs, out_specs=out_specs, check_vma=False)
```

time: 63.5 us -> 49.9 us (0.79)
  the two profiles are of different devices: /device:TPU:2 before, /device:TPU:18 now
where the time goes in v2:
time: 49.9 us; the launch traced here: 49.3 us
  Pallas kernels  48.4 us (97%)
  local copies, waits for them, and re-layouts  0.97 us (2%)
    pallas_call x1, Pallas kernels, local(): pl.pallas_call(kernel, out_shape=pltpu.VMEM((ROWS, 1024), BF16), in_specs...  48.4 us

profile of v2, /device:TPU:18, one launch (start us, length us, event | category | flops | bytes accessed | tf_op | source)
XLA Modules:
  0.0 49.3 jit_solution(12483111034682020092)
XLA Ops:
  0.0 48.4 %layer.1 = bf16[512,1024]{1,0:T(8,128)(2,1)S(1)} custom-call(bf16[512,4096]{1,0:T(8,128)(2,1)} %hid.1, bf16[4096,1024]{1,0:T(8,128)(2,1)} %wq.1, bf16[4096,256]{1,0:T(8,128)(2,1)} %wk.1, bf16[4096,256]{1,0:T(8,128)(2,1)} %wv.1, bf16[1024,4096]{1,0:T(8,128)(2,1)} %wo.1, f32[32,2,32,128]{3,2,1,0:T(8,128)} %constant.4.clone.coarse_tab, ...), custom_call_target="tpu_custom_call" | custom-call | tf_op jit(solution)/shard_map/layer/pallas_call | solution.py:507
  48.4 1.0 %copy.9 = bf16[512,1024]{1,0:T(8,128)(2,1)} copy(bf16[512,1024]{1,0:T(8,128)(2,1)S(1)} %layer.1) | data formatting | bytes 2097152

commit v3 on v2

--- a/solution.py
+++ b/solution.py
@@ -9,12 +9,23 @@
 HEAD = 128
 ROWS = 512
 WIDTH = 4096
-TILE = 128
-TILES = ROWS // TILE
+PART = 64
+PARTS = ROWS // PART
+TILES = ((0, 128), (128, 128), (256, 128), (384, 128))
+KROWS = 256
 CHUNKS = 2
 CROWS = ROWS // CHUNKS
 PIECE = CROWS // 8
-BODY = 256
+EARLY = ROWS - CROWS
+BODY = 4 * PART
+ROOT, PLACE, REST = range(3)
+PLAN = {
+    0: ((ROOT, 0, 0),),
+    1: ((ROOT, 1, 0), (REST, 0, 0)),
+    2: ((ROOT, 0, 1), (ROOT, 1, 1), (REST, 0, 1)),
+    3: ((PLACE, 0, 0), (PLACE, 1, 0)),
+    4: ((PLACE, 0, 1), (PLACE, 1, 1)),
+}
 MESH = pl.DeviceIdType.MESH
 LOW = -1e30
 F32 = jnp.float32
@@ -75,14 +86,14 @@
 
     hid_cp = [
         pltpu.make_async_copy(
-            hid.at[pl.ds(0, CROWS), pl.ds(d * 2048, 2048)],
-            hid_v.at[pl.ds(0, CROWS), pl.ds(d * 2048, 2048)],
+            hid.at[pl.ds(0, KROWS), pl.ds(d * 2048, 2048)],
+            hid_v.at[pl.ds(0, KROWS), pl.ds(d * 2048, 2048)],
             hid_sem.at[d],
         )
         for d in range(2)
     ]
     later_cp = pltpu.make_async_copy(
-        hid.at[pl.ds(CROWS, CROWS)], hid_v.at[pl.ds(CROWS, CROWS)], hid_sem.at[2]
+        hid.at[pl.ds(KROWS, KROWS)], hid_v.at[pl.ds(KROWS, KROWS)], hid_sem.at[2]
     )
     half = WIDTH // 2
     wkv_cp = [
@@ -126,7 +137,7 @@
 
         lax.fori_loop(0, ROWS // 16, step, 0, unroll=4)
 
-    scale = float(np.log2(np.e) / np.sqrt(HEAD))
+    scale = float(1 / np.sqrt(HEAD))
 
     def turn(x, c, s):
         return x * c + pltpu.roll(x, HEAD // 2, 1) * s
@@ -237,16 +248,23 @@
                 for ch in range(CHUNKS):
                     send_rest(ch, part)
 
-    def relay(ch, side, early):
+    def relay(early, ch, side):
         @pl.when(jnp.logical_and(xl == side, core == 1))
         def _():
             for part in range(2):
                 relay_part(ch, part, early)
 
+    def slot(k):
+        for what, ch, side in PLAN.get(k, ()):
+            if what == REST:
+                root_rest(side)
+            else:
+                relay(what == ROOT, ch, side)
+
     for cp in first_half:
         cp.wait()
-    for i in range(CHUNKS):
-        rows = pl.ds(i * CROWS, CROWS)
+    for i in range(ROWS // KROWS):
+        rows = pl.ds(i * KROWS, KROWS)
         if i == 0:
             kv_acc[...] = dot(hid_v[rows, 0:half], wkv_v[0:half, :])
             for cp in second_half:
@@ -286,8 +304,7 @@
     for cp in woa_cp + wob_cp:
         cp.start()
 
-    relay(0, 0, True)
-    relay(1, 0, True)
+    slot(0)
     for n in range(4):
         g, m = n // 2, n % 2
         if m == 0:
@@ -297,50 +314,41 @@
         c, s = cos_v[rows, :] * scale, sin_v[rows, :] * scale
         for j in range(4):
             turned = turn(x[:, j * HEAD : (j + 1) * HEAD], c, s).astype(BF16)
-            for tt in range(2):
-                q_v[(2 * m + tt) * 2 + g, j * TILE : (j + 1) * TILE, :] = turned[
-                    tt * TILE : (tt + 1) * TILE
+            for k in range(4):
+                q_v[(4 * m + k) * 2 + g, j * PART : (j + 1) * PART, :] = turned[
+                    k * PART : (k + 1) * PART
                 ]
-        if n == 1:
-            root_rest(0)
-        if n == 2:
-            relay(0, 1, True)
-            relay(1, 1, True)
-            relay(0, 0, False)
-            relay(1, 0, False)
-        if n == 3:
-            root_rest(1)
-
-    diag = lax.broadcasted_iota(jnp.int32, (BODY, TILE), 1) <= lax.rem(
-        lax.broadcasted_iota(jnp.int32, (BODY, TILE), 0), TILE
-    )
-    bodies = [(g, b) for g in range(2) for b in range(ROWS // BODY)]
-
-    def local_scores(t, g, b):
-        q = q_v[t * 2 + g, b * BODY : (b + 1) * BODY, :]
-        return dot_t(q, kvl[0 : (t + 1) * TILE, g * HEAD : (g + 1) * HEAD])
-
-    def local_finish(t, g, b, s):
-        rows = slice(b * BODY, (b + 1) * BODY)
-        last = jnp.where(diag, s[:, t * TILE :], LOW)
-        s = last if t == 0 else jnp.concatenate([s[:, : t * TILE], last], axis=1)
+        slot(n + 1)
+
+    row = lax.rem(lax.broadcasted_iota(jnp.int32, (BODY, HEAD), 0), PART)
+    col = lax.broadcasted_iota(jnp.int32, (BODY, HEAD), 1)
+    diag = (col <= row, col <= row + PART)
+
+    def in_turn(bodies, scores, finish):
+        every = [scores(*body) for body in bodies]
+        for body, s in zip(bodies, every):
+            finish(*body, s)
+
+    def bodies_of(t):
+        start, size = TILES[t]
+        return [(b, g) for g in range(2) for b in range(start // PART, (start + size) // PART)]
+
+    def local_scores(b, g):
+        keys = (b // 2 + 1) * HEAD
+        return dot_t(q_v[b * 2 + g], kvl[0:keys, g * HEAD : (g + 1) * HEAD])
+
+    def local_finish(b, g, s):
+        before = b // 2 * HEAD
+        last = jnp.where(diag[b % 2], s[:, before:], LOW)
+        s = jnp.concatenate([s[:, :before], last], axis=1) if before else last
         top = jnp.max(s, axis=1, keepdims=True)
-        p = jnp.exp2(s - top).astype(BF16)
-        ol[t * 2 + g, rows, :] = dot(p, vl_aug[g, 0 : (t + 1) * TILE, :])
-        ml[t * 2 + g, rows, :] = jnp.broadcast_to(top, (BODY, HEAD))
-
-    def local_tile(t):
-        s = local_scores(t, *bodies[0])
-        for k, (g, b) in enumerate(bodies):
-            ahead = local_scores(t, *bodies[k + 1]) if k + 1 < len(bodies) else None
-            local_finish(t, g, b, s)
-            s = ahead
-
-    local_tile(1)
-    local_tile(2)
-    relay(0, 1, False)
-    relay(1, 1, False)
-    local_tile(3)
+        p = jnp.exp(s - top).astype(BF16)
+        ol[b * 2 + g] = dot(p, vl_aug[g, 0 : before + HEAD, :])
+        ml[b * 2 + g] = jnp.broadcast_to(top, (BODY, HEAD))
+
+    for t in range(1, len(TILES)):
+        in_turn(bodies_of(t), local_scores, local_finish)
+        slot(4 + t)
 
     got, eight = pl.ds(0, 6 * PIECE), pl.ds(0, 8 * PIECE)
 
@@ -357,10 +365,13 @@
         for g in range(2):
             va_aug[g, rows, 0:HEAD] = kva[rows, 256 + g * HEAD : 256 + (g + 1) * HEAD]
 
+    def tile_rows(t):
+        return pl.ds(*TILES[t])
+
     def ctx_copy(t, g):
         cols = pl.ds(g * 512, 512)
         return pltpu.make_async_remote_copy(
-            src_ref=ctx.at[t, :, cols], dst_ref=ctx_sib.at[t, :, cols],
+            src_ref=ctx.at[tile_rows(t), cols], dst_ref=ctx_sib.at[tile_rows(t), cols],
             send_sem=ctx_send.at[t, g], recv_sem=ctx_recv.at[t, g],
             device_id=sibling, device_id_type=MESH,
         )
@@ -368,65 +379,63 @@
     def x_copy(t, c):
         cols = pl.ds(c * 512, 512)
         return pltpu.make_async_remote_copy(
-            src_ref=sbuf.at[t, :, cols], dst_ref=rbuf.at[t, :, cols],
+            src_ref=sbuf.at[tile_rows(t), cols], dst_ref=rbuf.at[tile_rows(t), cols],
             send_sem=x_send.at[t, c], recv_sem=x_recv.at[t, c],
             device_id=far, device_id_type=MESH,
         )
 
     has_anchor = blk > 0
 
-    def early_scores(g, b):
-        q = q_v[g, b * BODY : (b + 1) * BODY, :]
-        cols = slice(g * HEAD, (g + 1) * HEAD)
-        return dot_t(q, kva[0:CROWS, cols]), dot_t(q, kvl[0:TILE, cols])
-
-    def early_finish(g, b, s):
-        rows = slice(b * BODY, (b + 1) * BODY)
+    def early_scores(b, g):
+        q, cols = q_v[b * 2 + g], slice(g * HEAD, (g + 1) * HEAD)
+        return dot_t(q, kva[0:EARLY, cols]), dot_t(q, kvl[0:HEAD, cols])
+
+    def early_finish(b, g, s):
         s = jnp.concatenate(
-            [jnp.where(has_anchor, s[0], LOW), jnp.where(diag, s[1], LOW)], axis=1
+            [jnp.where(has_anchor, s[0], LOW), jnp.where(diag[b % 2], s[1], LOW)], axis=1
         )
         top = jnp.max(s, axis=1, keepdims=True)
-        p = jnp.exp2(s - top).astype(BF16)
-        ol[g, rows, :] = dot(p[:, 0:CROWS], va_aug[g, 0:CROWS, :]) + dot(
-            p[:, CROWS:], vl_aug[g, 0:TILE, :]
-        )
-        ml[g, rows, :] = jnp.broadcast_to(top, (BODY, HEAD))
-
-    anchor_here(0)
-    s = early_scores(*bodies[0])
-    for k, (g, b) in enumerate(bodies):
-        ahead = early_scores(*bodies[k + 1]) if k + 1 < len(bodies) else None
-        early_finish(g, b, s)
-        s = ahead
-    anchor_here(1)
-
-    def anchor_scores(t, g, b):
-        q = q_v[t * 2 + g, b * BODY : (b + 1) * BODY, :]
-        return dot_t(q, kva[0 if t else CROWS : ROWS, g * HEAD : (g + 1) * HEAD])
-
-    def anchor_finish(t, g, b, s):
-        rows = slice(b * BODY, (b + 1) * BODY)
-        before = ml[t * 2 + g, rows, :][:, 0:1]
+        p = jnp.exp(s - top).astype(BF16)
+        ol[b * 2 + g] = dot(p[:, 0:EARLY], va_aug[g, 0:EARLY, :]) + dot(
+            p[:, EARLY:], vl_aug[g, 0:HEAD, :]
+        )
+        ml[b * 2 + g] = jnp.broadcast_to(top, (BODY, HEAD))
+
+    for ch in range(CHUNKS - 1):
+        anchor_here(ch)
+    in_turn(bodies_of(0), early_scores, early_finish)
+    anchor_here(CHUNKS - 1)
+
+    def first_key(b):
+        return 0 if b * PART >= TILES[0][1] else EARLY
+
+    def anchor_scores(b, g):
+        return dot_t(q_v[b * 2 + g], kva[first_key(b) :, g * HEAD : (g + 1) * HEAD])
+
+    def anchor_finish(b, g, s):
+        before = ml[b * 2 + g][:, 0:1]
         both = jnp.maximum(jnp.max(s, axis=1, keepdims=True), before)
         top = jnp.where(has_anchor, both, before)
-        p = jnp.exp2(s - jnp.where(has_anchor, both, -LOW)).astype(BF16)
-        o = dot(p, va_aug[g, 0 if t else CROWS : ROWS, :]) + ol[t * 2 + g, rows, :] * jnp.exp2(before - top)
+        p = jnp.exp(s - jnp.where(has_anchor, both, -LOW)).astype(BF16)
+        o = dot(p, va_aug[g, first_key(b) :, :]) + ol[b * 2 + g] * jnp.exp(before - top)
         res = (o[:, 0:HEAD] / o[:, HEAD:]).astype(BF16)
-        for j in range(BODY // TILE):
-            col = (g * 4 + b * (BODY // TILE) + j) * HEAD
-            ctx[t, :, col : col + HEAD] = res[j * TILE : (j + 1) * TILE]
+        for j in range(4):
+            cols = slice((g * 4 + j) * HEAD, (g * 4 + j + 1) * HEAD)
+            ctx[b * PART : (b + 1) * PART, cols] = res[j * PART : (j + 1) * PART]
 
     def anchor_tile(t):
-        s = anchor_scores(t, *bodies[0])
-        for k, (g, b) in enumerate(bodies):
-            ahead = anchor_scores(t, *bodies[k + 1]) if k + 1 < len(bodies) else None
-            anchor_finish(t, g, b, s)
-            s = ahead
-            if b == ROWS // BODY - 1:
+        ends = TILES[t][0] + TILES[t][1] - PART
+
+        def finish(b, g, s):
+            anchor_finish(b, g, s)
+            if b * PART == ends:
                 ctx_copy(t, g).start()
 
-    def near_part(t):
-        acc_l[t] = dot(ctx[t], wo_a[1]) + dot(ctx_sib[t], wo_b[1])
+        in_turn(bodies_of(t), anchor_scores, finish)
+
+    def near_part(start):
+        rows = pl.ds(start, 256)
+        acc_l[rows, :] = dot(ctx[rows, :], wo_a[1]) + dot(ctx_sib[rows, :], wo_b[1])
 
     def sibling_here(t):
         for g in range(2):
@@ -435,33 +444,41 @@
     anchor_tile(0)
     for cp in woa_cp:
         cp.wait()
-    acc_r[...] = dot(ctx[0], wo_a[0])
+    head_rows = tile_rows(0)
+    acc_r[...] = dot(ctx[head_rows, :], wo_a[0])
     for cp in wob_cp:
         cp.wait_recv()
     sibling_here(0)
     for c in range(2):
         cols = slice(c * 512, (c + 1) * 512)
-        sbuf[0, :, cols] = (acc_r[:, cols] + dot(ctx_sib[0], wo_b[0, :, cols])).astype(BF16)
+        sbuf[head_rows, cols] = (
+            acc_r[:, cols] + dot(ctx_sib[head_rows, :], wo_b[0, :, cols])
+        ).astype(BF16)
         x_copy(0, c).start()
-    for t in range(1, TILES):
-        anchor_tile(t)
-        near_part(t - 1)
+    def far_part(t):
         sibling_here(t)
+        rows = tile_rows(t)
         for c in range(2):
             cols = slice(c * 512, (c + 1) * 512)
-            sbuf[t, :, cols] = (
-                dot(ctx[t], wo_a[0, :, cols]) + dot(ctx_sib[t], wo_b[0, :, cols])
+            sbuf[rows, cols] = (
+                dot(ctx[rows, :], wo_a[0, :, cols]) + dot(ctx_sib[rows, :], wo_b[0, :, cols])
             ).astype(BF16)
             x_copy(t, c).start()
-    near_part(TILES - 1)
-
-    for t in range(TILES):
+
+    for t in range(1, len(TILES)):
+        anchor_tile(t)
+        if t > 1:
+            far_part(t - 1)
+    far_part(len(TILES) - 1)
+    for start in range(0, ROWS, 256):
+        near_part(start)
+
+    for t in range(len(TILES)):
+        rows = tile_rows(t)
         for c in range(2):
             cols = slice(c * 512, (c + 1) * 512)
             x_copy(t, c).wait_recv()
-            out[pl.ds(t * TILE, TILE), cols] = (
-                acc_l[t, :, cols] + rbuf[t, :, cols].astype(F32)
-            ).astype(BF16)
+            out[rows, cols] = (acc_l[rows, cols] + rbuf[rows, cols].astype(F32)).astype(BF16)
 
     for cp in wob_cp:
         cp.wait_send()
@@ -494,7 +511,7 @@
             for grp in range(2):
                 pltpu.make_async_copy(kva.at[got], kva.at[got], rest_send.at[ch, grp]).wait()
 
-    for t in range(TILES):
+    for t in range(len(TILES)):
         for g in range(2):
             ctx_copy(t, g).wait_send()
             x_copy(t, g).wait_send()
@@ -519,25 +536,26 @@
             pltpu.VMEM((2, 16, HEAD), F32),
             pltpu.VMEM((ROWS, HEAD), F32),
             pltpu.VMEM((ROWS, HEAD), F32),
-            pltpu.VMEM((CROWS, 512), F32),
+            pltpu.VMEM((KROWS, 512), F32),
             pltpu.VMEM((ROWS, 512), BF16),
             pltpu.VMEM((ROWS, 512), BF16),
             pltpu.VMEM((ROWS, 512), BF16),
-            pltpu.VMEM((TILES * 2, 4 * TILE, HEAD), BF16),
+            pltpu.VMEM((PARTS * 2, BODY, HEAD), BF16),
             pltpu.VMEM((2, ROWS, 2 * HEAD), BF16),
             pltpu.VMEM((2, ROWS, 2 * HEAD), BF16),
-            pltpu.VMEM((TILES * 2, 4 * TILE, 2 * HEAD), F32),
-            pltpu.VMEM((TILES * 2, 4 * TILE, HEAD), F32),
-            pltpu.VMEM((TILES, TILE, 1024), BF16),
-            pltpu.VMEM((TILES, TILE, 1024), BF16),
-            pltpu.VMEM((TILE, 1024), F32),
-            pltpu.VMEM((TILES, TILE, 1024), F32),
-            pltpu.VMEM((TILES, TILE, 1024), BF16),
-            pltpu.VMEM((TILES, TILE, 1024), BF16),
+            pltpu.VMEM((PARTS * 2, BODY, 2 * HEAD), F32),
+            pltpu.VMEM((PARTS * 2, BODY, HEAD), F32),
+            pltpu.VMEM((ROWS, 1024), BF16),
+            pltpu.VMEM((ROWS, 1024), BF16),
+            pltpu.VMEM((TILES[0][1], 1024), F32),
+            pltpu.VMEM((ROWS, 1024), F32),
+            pltpu.VMEM((ROWS, 1024), BF16),
+            pltpu.VMEM((ROWS, 1024), BF16),
             dma((3,)), dma((2, 2)), dma((2,)), dma((2,)), dma((2,)), dma((2,)), dma((2,)),
             dma((CHUNKS,)), dma((CHUNKS, 2)), dma((CHUNKS, 2, 2)), dma((CHUNKS, 2, 2)),
             dma((CHUNKS, 2, 2)), dma((CHUNKS, 2)), dma((CHUNKS, 2)), dma((CHUNKS,)),
-            dma((TILES, 2)), dma((TILES, 2)), dma((TILES, 2)), dma((TILES, 2)),
+            dma((len(TILES), 2)), dma((len(TILES), 2)),
+            dma((len(TILES), 2)), dma((len(TILES), 2)),
             dma((CHUNKS, 2)),
         ],
         compiler_params=pltpu.CompilerParams(

time: 49.9 us -> 49.2 us (0.986); the launches traced: 49.3 us -> 49.1 us
  no operation moved by 1% of the time
where the time goes in v3:
time: 49.2 us; the launch traced here: 49.1 us
  Pallas kernels  48.2 us (98%)
  local copies, waits for them, and re-layouts  0.97 us (2%)
    pallas_call x1, Pallas kernels, local(): pl.pallas_call(kernel, out_shape=pltpu.VMEM((ROWS, 1024), BF16), in_specs...  48.2 us

profile of v3, /device:TPU:18, one launch (start us, length us, event | category | flops | bytes accessed | tf_op | source)
XLA Modules:
  0.0 49.1 jit_solution(14003549099833558015)
XLA Ops:
  0.0 48.2 %layer.1 = bf16[512,1024]{1,0:T(8,128)(2,1)S(1)} custom-call(bf16[512,4096]{1,0:T(8,128)(2,1)} %hid.1, bf16[4096,1024]{1,0:T(8,128)(2,1)} %wq.1, bf16[4096,256]{1,0:T(8,128)(2,1)} %wk.1, bf16[4096,256]{1,0:T(8,128)(2,1)} %wv.1, bf16[1024,4096]{1,0:T(8,128)(2,1)} %wo.1, f32[32,2,32,128]{3,2,1,0:T(8,128)} %constant.4.clone.coarse_tab, ...), custom_call_target="tpu_custom_call" | custom-call | tf_op jit(solution)/shard_map/layer/pallas_call | solution.py:524
  48.2 1.0 %copy.9 = bf16[512,1024]{1,0:T(8,128)(2,1)} copy(bf16[512,1024]{1,0:T(8,128)(2,1)S(1)} %layer.1) | data formatting | bytes 2097152

commit v4 on v3

--- a/solution.py
+++ b/solution.py
@@ -55,9 +55,8 @@
     hid, wq, wk, wv, wo, coarse_tab, fine_tab, out,
     hid_v, wq_v, wkv_v, wo_a, wo_b, coarse, fine, cos_v, sin_v,
     kv_acc, kvl, kva, stage, q_v, vl_aug, va_aug, ol, ml, ctx, ctx_sib, acc_r, acc_l, sbuf, rbuf,
-    hid_sem, wkv_sem, tab_sem, wq_sem, woa_sem, wob_send, wob_recv,
-    first_send, aside_send, mine_recv, ring_send, fwd_send, rest_send, home_send, rest_recv,
-    ctx_send, ctx_recv, x_send, x_recv, own_sem,
+    load_sem, wob_send, wob_recv, first_send, mine_recv, ring_send, rest_send, rest_recv,
+    ctx_send, ctx_recv, x_send, x_recv,
 ):
     blk = lax.axis_index("blk")
     head = lax.axis_index("head")
@@ -88,37 +87,41 @@
         pltpu.make_async_copy(
             hid.at[pl.ds(0, KROWS), pl.ds(d * 2048, 2048)],
             hid_v.at[pl.ds(0, KROWS), pl.ds(d * 2048, 2048)],
-            hid_sem.at[d],
+            load_sem.at[d],
         )
         for d in range(2)
     ]
     later_cp = pltpu.make_async_copy(
-        hid.at[pl.ds(KROWS, KROWS)], hid_v.at[pl.ds(KROWS, KROWS)], hid_sem.at[2]
+        hid.at[pl.ds(KROWS, KROWS)], hid_v.at[pl.ds(KROWS, KROWS)], load_sem.at[2]
     )
     half = WIDTH // 2
     wkv_cp = [
         pltpu.make_async_copy(
             w.at[pl.ds(d * half, half)],
             wkv_v.at[pl.ds(d * half, half), pl.ds(i * 256, 256)],
-            wkv_sem.at[d, i],
+            load_sem.at[d],
         )
         for d in range(2)
         for i, w in enumerate((wk, wv))
     ]
     tab_cp = [
-        pltpu.make_async_copy(coarse_tab.at[blk], coarse, tab_sem.at[0]),
-        pltpu.make_async_copy(fine_tab, fine, tab_sem.at[1]),
+        pltpu.make_async_copy(coarse_tab.at[blk], coarse, load_sem.at[3]),
+        pltpu.make_async_copy(fine_tab, fine, load_sem.at[3]),
     ]
     wq_cp = [
-        pltpu.make_async_copy(wq.at[:, pl.ds(n * 512, 512)], wq_v.at[n], wq_sem.at[n])
+        pltpu.make_async_copy(wq.at[:, pl.ds(n * 512, 512)], wq_v.at[n], load_sem.at[n])
         for n in range(2)
     ]
     woa_cp = [
         pltpu.make_async_copy(
-            wo.at[:, pl.ds(pl.multiple_of(h * 1024, 1024), 1024)], wo_a.at[i], woa_sem.at[i]
+            wo.at[:, pl.ds(pl.multiple_of(h * 1024, 1024), 1024)], wo_a.at[i], load_sem.at[2]
         )
         for i, h in enumerate((far_head, head))
     ]
+
+    def wait_all(like, sem):
+        pltpu.make_async_copy(like, like, sem).wait()
+
     first_half = [hid_cp[0], wkv_cp[0], wkv_cp[1]]
     second_half = [hid_cp[1], wkv_cp[2], wkv_cp[3]]
     for cp in tab_cp + first_half + second_half + [later_cp]:
@@ -155,42 +158,38 @@
             device_id=target, device_id_type=MESH,
         )
 
-    def own_copy(ch, part):
-        rows = piece(ch, part, 0)
-        return pltpu.make_async_copy(kvl.at[rows], kva.at[rows], own_sem.at[ch, part])
-
     def aside(ch, part):
         return push(
-            kvl, stage, ch, part, 0, aside_send.at[ch, part], mine_recv.at[ch, part, 0], sibling
+            kvl, stage, ch, part, 0, first_send, mine_recv.at[ch, part], sibling
         )
 
     def first(ch, part, d, grp):
         return push(
-            kvl, held[grp], ch, part, d, first_send.at[ch], mine_recv.at[ch, part, grp],
+            kvl, held[grp], ch, part, d, first_send, mine_recv.at[ch, part],
             (rings[part][d - 1], one),
         )
 
     def forward(ch, part, grp):
         return push(
-            held[grp], held[grp], ch, part, lines[part], fwd_send.at[ch, part, grp],
-            mine_recv.at[ch, part, grp], (xl_peer, one),
+            held[grp], held[grp], ch, part, lines[part], ring_send.at[part],
+            mine_recv.at[ch, part], (xl_peer, one),
         )
 
     def across(ch, part, d, grp):
         return push(
-            held[grp], held[grp], ch, part, lines[part], ring_send.at[ch, part, grp],
-            mine_recv.at[ch, part, grp], (rings[1 - part][d - 1], one),
+            held[grp], held[grp], ch, part, lines[part], ring_send.at[part],
+            mine_recv.at[ch, part], (rings[1 - part][d - 1], one),
         )
 
     def rest(ch, part, d, grp):
         return push(
-            held[grp], kva, ch, part, lines[part], rest_send.at[ch, grp], rest_recv.at[ch],
+            held[grp], kva, ch, part, lines[part], rest_send, rest_recv.at[ch],
             (rings[part][d - 1], (zero, one)[grp]),
         )
 
     def home(ch, part):
         return push(
-            stage, kva, ch, part, lines[part], home_send.at[ch, part], rest_recv.at[ch], sibling
+            stage, kva, ch, part, lines[part], rest_send, rest_recv.at[ch], sibling
         )
 
     def scatter_chunk(ch):
@@ -198,44 +197,42 @@
             @pl.when(jnp.logical_and(blk == 0, core == grp))
             def _(grp=grp):
                 for part in range(2):
-                    for d in (1, 2, 3):
+                    for d in (2, 1, 3):
                         first(ch, part, d, grp).start()
                 for part in range(2):
                     if grp == 0:
                         aside(ch, part).start()
                     else:
-                        own_copy(ch, part).start()
+                        start = ch * CROWS + part * 4 * PIECE
+                        kva[start : start + PIECE, :] = kvl[start : start + PIECE, :]
 
     def relay_part(ch, part, early):
         at_root = lines[1 - part] == 0
 
         @pl.when(at_root if early else jnp.logical_not(at_root))
         def _():
-            forward(ch, part, 0).wait_recv()
-            if early:
-                @pl.when(blk == 0)
-                def _():
-                    own_copy(ch, part).wait()
-
-                @pl.when(blk != 0)
-                def _():
-                    forward(ch, part, 1).wait_recv()
-            else:
-                forward(ch, part, 1).wait_recv()
+            @pl.when(blk == 0)
+            def _():
+                wait_all(kva.at[pl.ds(0, PIECE)], mine_recv.at[ch, part])
+
+            @pl.when(blk != 0)
+            def _():
+                wait_all(kva.at[pl.ds(0, 2 * PIECE)], mine_recv.at[ch, part])
+
             if early:
                 for grp in range(2):
                     @pl.when(xl == 0)
                     def _(grp=grp):
                         forward(ch, part, grp).start()
 
-                    for d in (1, 2, 3):
+                    for d in (2, 1, 3):
                         across(ch, part, d, grp).start()
             else:
                 send_rest(ch, part)
 
     def send_rest(ch, part):
         for grp in range(2):
-            for d in (1, 2, 3):
+            for d in (2, 1, 3):
                 rest(ch, part, d, grp).start()
         home(ch, part).start()
 
@@ -261,19 +258,16 @@
             else:
                 relay(what == ROOT, ch, side)
 
-    for cp in first_half:
-        cp.wait()
+    wait_all(hid_v.at[pl.ds(0, 384)], load_sem.at[0])
     for i in range(ROWS // KROWS):
         rows = pl.ds(i * KROWS, KROWS)
         if i == 0:
             kv_acc[...] = dot(hid_v[rows, 0:half], wkv_v[0:half, :])
-            for cp in second_half:
-                cp.wait()
+            wait_all(hid_v.at[pl.ds(0, 384)], load_sem.at[1])
             for cp in wq_cp:
                 cp.start()
             kv_acc[...] += dot(hid_v[rows, half:], wkv_v[half:, :])
-            for cp in tab_cp:
-                cp.wait()
+            wait_all(cos_v.at[pl.ds(0, 96)], load_sem.at[3])
             make_tables()
             kv = kv_acc[...]
         else:
@@ -296,7 +290,7 @@
     wob_cp = [
         pltpu.make_async_remote_copy(
             src_ref=wo.at[:, pl.ds(pl.multiple_of(h * 1024, 1024), 1024)], dst_ref=wo_b.at[i],
-            send_sem=wob_send.at[i], recv_sem=wob_recv.at[i],
+            send_sem=wob_send, recv_sem=wob_recv,
             device_id=sibling, device_id_type=MESH,
         )
         for i, h in enumerate(((1 - xh) * 2 + other, xh * 2 + other))
@@ -368,19 +362,18 @@
     def tile_rows(t):
         return pl.ds(*TILES[t])
 
-    def ctx_copy(t, g):
-        cols = pl.ds(g * 512, 512)
+    def ctx_copy(t):
+        rows = tile_rows(t)
         return pltpu.make_async_remote_copy(
-            src_ref=ctx.at[tile_rows(t), cols], dst_ref=ctx_sib.at[tile_rows(t), cols],
-            send_sem=ctx_send.at[t, g], recv_sem=ctx_recv.at[t, g],
-            device_id=sibling, device_id_type=MESH,
+            src_ref=ctx.at[rows], dst_ref=ctx_sib.at[rows], send_sem=ctx_send,
+            recv_sem=ctx_recv.at[t], device_id=sibling, device_id_type=MESH,
         )
 
     def x_copy(t, c):
         cols = pl.ds(c * 512, 512)
         return pltpu.make_async_remote_copy(
             src_ref=sbuf.at[tile_rows(t), cols], dst_ref=rbuf.at[tile_rows(t), cols],
-            send_sem=x_send.at[t, c], recv_sem=x_recv.at[t, c],
+            send_sem=x_send, recv_sem=x_recv.at[t],
             device_id=far, device_id_type=MESH,
         )
 
@@ -424,30 +417,21 @@
             ctx[b * PART : (b + 1) * PART, cols] = res[j * PART : (j + 1) * PART]
 
     def anchor_tile(t):
-        ends = TILES[t][0] + TILES[t][1] - PART
-
-        def finish(b, g, s):
-            anchor_finish(b, g, s)
-            if b * PART == ends:
-                ctx_copy(t, g).start()
-
-        in_turn(bodies_of(t), anchor_scores, finish)
+        in_turn(bodies_of(t), anchor_scores, anchor_finish)
+        ctx_copy(t).start()
 
     def near_part(start):
         rows = pl.ds(start, 256)
         acc_l[rows, :] = dot(ctx[rows, :], wo_a[1]) + dot(ctx_sib[rows, :], wo_b[1])
 
     def sibling_here(t):
-        for g in range(2):
-            ctx_copy(t, g).wait_recv()
+        wait_all(ctx_sib.at[tile_rows(t)], ctx_recv.at[t])
 
     anchor_tile(0)
-    for cp in woa_cp:
-        cp.wait()
+    wait_all(wo_a, load_sem.at[2])
     head_rows = tile_rows(0)
     acc_r[...] = dot(ctx[head_rows, :], wo_a[0])
-    for cp in wob_cp:
-        cp.wait_recv()
+    wait_all(wo_b, wob_recv)
     sibling_here(0)
     for c in range(2):
         cols = slice(c * 512, (c + 1) * 512)
@@ -475,46 +459,27 @@
 
     for t in range(len(TILES)):
         rows = tile_rows(t)
-        for c in range(2):
-            cols = slice(c * 512, (c + 1) * 512)
-            x_copy(t, c).wait_recv()
-            out[rows, cols] = (acc_l[rows, cols] + rbuf[rows, cols].astype(F32)).astype(BF16)
-
-    for cp in wob_cp:
-        cp.wait_send()
-    for ch in range(CHUNKS):
-        @pl.when(blk == 0)
-        def _(ch=ch):
-            pltpu.make_async_copy(kvl.at[got], kvl.at[got], first_send.at[ch]).wait()
-
-            @pl.when(core == 0)
-            def _():
-                for part in range(2):
-                    aside(ch, part).wait_send()
-
-        @pl.when(core == 1)
-        def _(ch=ch):
-            for part in range(2):
-                @pl.when(lines[1 - part] == 0)
-                def _(part=part):
-                    three = pl.ds(0, 3 * PIECE)
-                    for grp in range(2):
-                        pltpu.make_async_copy(
-                            kva.at[three], kva.at[three], ring_send.at[ch, part, grp]
-                        ).wait()
-
-                        @pl.when(xl == 0)
-                        def _(grp=grp):
-                            forward(ch, part, grp).wait_send()
-
-                home(ch, part).wait_send()
-            for grp in range(2):
-                pltpu.make_async_copy(kva.at[got], kva.at[got], rest_send.at[ch, grp]).wait()
-
-    for t in range(len(TILES)):
-        for g in range(2):
-            ctx_copy(t, g).wait_send()
-            x_copy(t, g).wait_send()
+        wait_all(rbuf.at[rows], x_recv.at[t])
+        out[rows, :] = (acc_l[rows, :] + rbuf[rows, :].astype(F32)).astype(BF16)
+
+    wait_all(wo_b, wob_send)
+    for grp, pieces in ((0, 8 * CHUNKS), (1, 6 * CHUNKS)):
+        @pl.when(jnp.logical_and(blk == 0, core == grp))
+        def _(pieces=pieces):
+            wait_all(kva.at[pl.ds(0, pieces * PIECE)], first_send)
+
+    @pl.when(core == 1)
+    def _():
+        for part in range(2):
+            for side, pieces in ((0, 8 * CHUNKS), (1, 6 * CHUNKS)):
+                @pl.when(jnp.logical_and(lines[1 - part] == 0, xl == side))
+                def _(part=part, pieces=pieces):
+                    wait_all(kva.at[pl.ds(0, pieces * PIECE)], ring_send.at[part])
+
+        wait_all(hid_v.at[pl.ds(0, 14 * CHUNKS * PIECE // 8)], rest_send)
+
+    wait_all(ctx, ctx_send)
+    wait_all(sbuf, x_send)
 
 
 def local(hidden_states, w_query, key_matrix, value_matrix, w_out):
@@ -551,12 +516,9 @@
             pltpu.VMEM((ROWS, 1024), F32),
             pltpu.VMEM((ROWS, 1024), BF16),
             pltpu.VMEM((ROWS, 1024), BF16),
-            dma((3,)), dma((2, 2)), dma((2,)), dma((2,)), dma((2,)), dma((2,)), dma((2,)),
-            dma((CHUNKS,)), dma((CHUNKS, 2)), dma((CHUNKS, 2, 2)), dma((CHUNKS, 2, 2)),
-            dma((CHUNKS, 2, 2)), dma((CHUNKS, 2)), dma((CHUNKS, 2)), dma((CHUNKS,)),
-            dma((len(TILES), 2)), dma((len(TILES), 2)),
-            dma((len(TILES), 2)), dma((len(TILES), 2)),
-            dma((CHUNKS, 2)),
+            dma((4,)), dma, dma,
+            dma, dma((CHUNKS, 2)), dma((2,)), dma, dma((CHUNKS,)),
+            dma, dma((len(TILES),)), dma, dma((len(TILES),)),
         ],
         compiler_params=pltpu.CompilerParams(
             collective_id=0, has_side_effects=True, vmem_limit_bytes=60 * 2**20

time: 49.2 us -> 48 us (0.976); the launches traced: 49.1 us -> 47.2 us
  Pallas kernels: 48.2 us -> 46.3 us
    pallas_call x1, Pallas kernels: 48.2 us -> 46.3 us  [local(): pl.pallas_call(kernel, out_shape=pltpu.VMEM((ROWS, 1024), BF16), in_specs...]
where the time goes in v4:
time: 48 us; the launch traced here: 47.2 us
  Pallas kernels  46.3 us (96%)
  local copies, waits for them, and re-layouts  0.97 us (2%)
    pallas_call x1, Pallas kernels, local(): pl.pallas_call(kernel, out_shape=pltpu.VMEM((ROWS, 1024), BF16), in_specs...  46.3 us
    unnamed x1, local copies, waits for them, and re-layouts  0.97 us

profile of v4, /device:TPU:18, one launch (start us, length us, event | category | flops | bytes accessed | tf_op | source)
XLA Modules:
  0.0 47.2 jit_solution(17085622888814169267)
XLA Ops:
  0.0 46.3 %layer.1 = bf16[512,1024]{1,0:T(8,128)(2,1)S(1)} custom-call(bf16[512,4096]{1,0:T(8,128)(2,1)} %hid.1, bf16[4096,1024]{1,0:T(8,128)(2,1)} %wq.1, bf16[4096,256]{1,0:T(8,128)(2,1)} %wk.1, bf16[4096,256]{1,0:T(8,128)(2,1)} %wv.1, bf16[1024,4096]{1,0:T(8,128)(2,1)} %wo.1, f32[32,2,32,128]{3,2,1,0:T(8,128)} %constant.4.clone.coarse_tab, ...), custom_call_target="tpu_custom_call" | custom-call | tf_op jit(solution)/shard_map/layer/pallas_call | solution.py:489
  46.3 1.0 %copy.9 = bf16[512,1024]{1,0:T(8,128)(2,1)} copy(bf16[512,1024]{1,0:T(8,128)(2,1)S(1)} %layer.1) | data formatting | bytes 2097152
